TPU v7x, 32 devices: a whole 2x2x4 slice. The times are simulated.
32 devices in a mesh: groups: 2 (over y), col: 4 (over x, core), row: 4 (over z).
Axes of the slice: x: 2, y: 2, z: 4, core: 2. Of those that a mesh axis runs over, the one named last changes fastest.
Arguments:
- right_vectors: bfloat16 [128, 32768], P('groups', ('col', 'row')), parts along dimension 0, may hold values from -6 to 6
- left_vectors: bfloat16 [128, 8192], P('groups', ('row', 'col')), parts along dimension 0, may hold values from -6 to 6
- diag_tiles: bfloat16 [16384, 2048], P(('groups', 'row', 'col')), parts along dimension 0, may hold values from -0.125 to 0.125
- tile_ranks: int32 [8, 16], P('groups', 'col'), parts along dimension 0, may hold values from 20 to 400, as said below
- tile_order: int32 [8, 16], P(('groups', 'col')), parts along dimension 0, may hold values from 0 to 15, each once within a row
- v_panels: bfloat16 [320, 128, 2048], P(('groups', 'col', 'row')), parts along dimension 0, may hold values from -0.25 to 0.25
- u_panels: bfloat16 [320, 128, 2048], P(('groups', 'col', 'row')), parts along dimension 0, may hold values from -0.1875 to 0.1875
Outputs:
- product_rows: bfloat16 [128, 8192], P('groups', ('row', 'col')), parts along dimension 0
- product_cols: bfloat16 [128, 32768], P('groups', ('col', 'row')), parts along dimension 0
There are 2 independent parts, one for each index of `groups`. A program takes and returns all parts, laid end to end along the dimension named above; each array names one. Nothing has to cross between parts.
Inputs may be any that keep to these rules, and one draw needn't show every extreme that they name: `tile_ranks`: in every column group the off-diagonal tiles together need at most 40 panels; entries of diagonal tiles are not read. `tile_order`: each row lists the 16 positions of one group once.
All inputs are finite; a program needn't handle non-finite values.
Results may differ from a plain program's by a relative error of at most 0.005.
Values may be sent and summed in bfloat16 or wider, within the bound.
A program may use at most 128 MiB of HBM per device.

v0:
```python
import jax
import jax.numpy as jnp
from jax import lax
from jax.sharding import PartitionSpec as P

PANEL = 128


def spread(shard, axis, root):
    mine = lax.axis_index(axis) == root
    return lax.psum(jnp.where(mine, shard, jnp.zeros_like(shard)), axis)


def panel_layout(ranks_group, order_group, group_index, helper, slot_count, row_count):
    per_group = ranks_group.shape[1]
    tile_count = row_count * per_group
    positions = jnp.arange(tile_count, dtype=jnp.int32)
    tile_rows = positions // per_group
    tile_cols = positions % per_group
    on_diagonal = tile_rows == group_index * per_group + tile_cols
    flat_ranks = ranks_group.reshape(tile_count)
    needed = jnp.where(on_diagonal, 0, (flat_ranks + PANEL - 1) // PANEL)
    listing = (order_group[:, None] == positions[None, :]).astype(jnp.int32)
    listed = jnp.sum(listing * needed[None, :], axis=1)
    starts = jnp.cumsum(listed) - listed
    slot_ids = helper * slot_count + jnp.arange(slot_count, dtype=jnp.int32)
    inside = (
        (slot_ids[:, None] >= starts[None, :]) & (slot_ids[:, None] < (starts + listed)[None, :])
    ).astype(jnp.int32)
    tile_hot = jnp.sum(inside[:, :, None] * listing[None, :, :], axis=1)
    panel_number = slot_ids - jnp.sum(inside * starts[None, :], axis=1)
    slot_ranks = jnp.sum(tile_hot * flat_ranks[None, :], axis=1)
    widths = jnp.clip(slot_ranks - panel_number * PANEL, 0, PANEL)
    valid_mask = (jnp.arange(PANEL, dtype=jnp.int32)[None, :] < widths[:, None]).astype(jnp.float32)
    shaped = tile_hot.reshape(slot_count, row_count, per_group)
    row_hot = jnp.sum(shaped, axis=2).astype(jnp.float32)
    col_hot = jnp.sum(shaped, axis=1).astype(jnp.float32)
    return (row_hot, col_hot, valid_mask)


def body(right_vectors, left_vectors, diag_tiles, tile_ranks, tile_order, v_panels, u_panels):
    highest = lax.Precision.HIGHEST
    row_count = lax.axis_size("row")
    col_count = lax.axis_size("col")
    group_index = lax.axis_index("col")
    helper = lax.axis_index("row")
    vec_count = right_vectors.shape[0]
    slot_count = v_panels.shape[0]
    tile_width = v_panels.shape[2]
    per_group = tile_ranks.shape[1]
    sub_width = tile_width // col_count
    row_hot, col_hot, valid_mask = panel_layout(
        tile_ranks, tile_order[0], group_index, helper, slot_count, row_count
    )
    gathered_x = lax.all_gather(right_vectors, "row", axis=1, tiled=True)
    x_blocks = gathered_x.reshape(vec_count, per_group, tile_width)
    picked_x = jnp.einsum(
        "pb,vbn->pvn", col_hot.astype(jnp.bfloat16), x_blocks, preferred_element_type=jnp.float32
    ).astype(jnp.bfloat16)
    coefficients = jnp.einsum(
        "pkn,pvn->pvk", v_panels, picked_x, preferred_element_type=jnp.float32
    )
    coefficients = (coefficients * valid_mask[:, None, :]).astype(jnp.bfloat16)
    products = jnp.einsum(
        "pvk,pkn->pvn", coefficients, u_panels, preferred_element_type=jnp.float32
    )
    products = products.reshape(slot_count, vec_count, col_count, sub_width)
    partial_value = jnp.einsum("pi,pvcw->civw", row_hot, products, precision=highest)
    reduced = lax.psum_scatter(
        partial_value.reshape(col_count * row_count, vec_count, sub_width),
        ("col", "row"),
        scatter_dimension=0,
        tiled=True,
    )
    own_block = lax.dynamic_slice_in_dim(gathered_x, helper % per_group * tile_width, tile_width, 1)
    diag_vector = spread(own_block, "col", helper // per_group)
    diag_part = jnp.einsum("vn,wn->vw", diag_vector, diag_tiles, preferred_element_type=jnp.float32)
    product_rows = (reduced.reshape(vec_count, sub_width) + diag_part).astype(jnp.bfloat16)
    row_hot_narrow = row_hot.astype(jnp.bfloat16)
    gathered_w = lax.all_gather(left_vectors, ("col", "row"), axis=1, tiled=True)
    gathered_w = gathered_w.reshape(vec_count, col_count, row_count, sub_width)
    picked_w = jnp.einsum(
        "pi,vciw->pvcw", row_hot_narrow, gathered_w, preferred_element_type=jnp.float32
    )
    picked_w = picked_w.reshape(slot_count, vec_count, tile_width).astype(jnp.bfloat16)
    transposed = jnp.einsum("pkn,pvn->pvk", u_panels, picked_w, preferred_element_type=jnp.float32)
    transposed = (transposed * valid_mask[:, None, :]).astype(jnp.bfloat16)
    returned = jnp.einsum("pvk,pkn->pvn", transposed, v_panels, preferred_element_type=jnp.float32)
    column_part = jnp.einsum("pb,pvn->vbn", col_hot, returned, precision=highest)
    column_part = column_part.reshape(vec_count, per_group * tile_width)
    product_cols = lax.psum_scatter(column_part, "row", scatter_dimension=1, tiled=True).astype(
        jnp.bfloat16
    )
    return (product_rows, product_cols)


def solution(mesh):
    in_specs = (
        P("groups", ("col", "row")),
        P("groups", ("row", "col")),
        P(("groups", "row", "col"), None),
        P("groups", "col"),
        P(("groups", "col"), None),
        P(("groups", "col", "row"), None, None),
        P(("groups", "col", "row"), None, None),
    )
    out_specs = (P("groups", ("row", "col")), P("groups", ("col", "row")))
    return jax.shard_map(body, mesh=mesh, in_specs=in_specs, out_specs=out_specs, check_vma=False)
```

profile of v0, /device:TPU:0, one launch (start us, length us, event | category | flops | bytes accessed | tf_op | source)
XLA Modules:
  0.0 232.0 jit_solution(803503507608508200)
XLA Ops:
  7.2 0.0 copy-start
  7.2 0.0 all-gather.3.cloned.1.call-start
  7.2 0.7 all-gather.3.cloned.1.call-update
  7.9 0.0 all-gather.5.cloned.1.call-start
  8.0 0.7 all-gather.5.cloned.1.call-update
  8.7 0.0 all-reduce.2.cloned.1.call-start
  8.7 0.7 fusion.33
  9.5 0.8 reshape.208
  10.2 0.8 select_reduce_fusion.1
  11.1 0.1 copy.16
  11.2 0.1 reduce
  11.3 0.1 fusion.35
  11.4 0.1 multiply_reduce_fusion
  11.5 0.1 copy.17
  11.6 0.1 multiply_reduce_fusion.1
  11.8 0.2 select_reduce_fusion
  11.9 0.1 fusion.34
  12.0 28.2 %all-gather.3.cloned.1.call-done = bf16[64,8192]{1,0:T(8,128)(2,1)} async-done(((bf16[64,2048]{1,0:T(8,128)(2,1)}), bf16[64,8192]{1,0:T(8,128)(2,1)}) %all-gather.3.cloned.1.call-update) | async-done | bytes 1048592 | tf_op jit(solution)/shard_map/all_gather | solution.py:55
  40.2 1.8 reshape.212
  42.1 3.0 %convolution_convert_fusion.1 = bf16[10,64,2048]{2,0,1:T(8,128)(2,1)} fusion(bf16[64,4,2048]{2,1,0:T(4,128)(2,1)S(1)} %reshape.212, s32[10,4]{0,1:T(4,128)S(1)} %get-tuple-element.3), kind=kOutput, calls=%fused_computation.5 | convolution fusion | flops 11796560 | bytes 3670176 | tf_op jit(solution)/shard_map/pb,vbn->pvn/dot_general | solution.py:57
  45.1 10.5 %fusion.27 = f32[10,64,2048]{2,1,0:T(8,128)} fusion(bf16[10,128,2048]{2,1,0:T(8,128)(2,1)} %param.13, bf16[10,128,2048]{2,1,0:T(8,128)(2,1)} %param.12, bf16[10,64,2048]{2,0,1:T(8,128)(2,1)} %convolution_convert_fusion.1, f32[10,128]{1,0:T(8,128)S(1)} %fusion.34), kind=kOutput, calls=%fused_computation.16 | convolution fusion | flops 671252480 | bytes 18355200 | tf_op jit(solution)/shard_map/pvk,pkn->pvn/dot_general | solution.py:64
  55.6 7.6 %reshape.213 = f32[10,64,4,512]{3,2,1,0:T(4,128)} reshape(f32[10,64,2048]{2,1,0:T(8,128)} %fusion.27) | data formatting | bytes 10485760 | tf_op jit(solution)/shard_map/reshape | solution.py:67
  63.1 1.7 dynamic-slice_select_fusion
  64.8 0.0 all-reduce.2.cloned.1.call-update
  64.9 0.2 reduce-scatter.3.cloned.1.call-start
  65.1 13.1 %fusion.8 = f32[4,4,64,512]{3,1,0,2:T(4,128)S(1)} fusion(f32[10,64,4,512]{3,2,1,0:T(4,128)} %reshape.213, s32[10,4]{0,1:T(4,128)S(1)} %get-tuple-element.2), kind=kOutput, calls=%fused_computation.10 | convolution fusion | flops 62914600 | bytes 7340192 | tf_op jit(solution)/shard_map/pi,pvcw->civw/dot_general | solution.py:68
  78.2 2.5 %copy.26 = f32[4,4,64,512]{3,2,1,0:T(8,128)} copy(f32[4,4,64,512]{3,1,0,2:T(4,128)S(1)} %fusion.8) | data formatting | bytes 4194304 | tf_op jit(solution)/shard_map/reshape | solution.py:70
  80.7 0.0 reduce-scatter.3.cloned.1.call-update
  80.7 0.3 reduce-scatter.5.cloned.1.call-start
  81.0 0.0 all-gather.5.cloned.1.call-done
  81.0 1.8 reshape.216
  82.9 1.4 copy.53
  84.3 1.8 dot_general.37
  86.1 3.0 %convolution_convert_fusion = bf16[10,64,2048]{2,0,1:T(8,128)(2,1)} fusion(bf16[64,2048,4]{1,0,2:T(8,128)(2,1)S(1)} %dot_general.37, s32[10,4]{0,1:T(4,128)S(1)} %get-tuple-element.2), kind=kOutput, calls=%fused_computation.4 | convolution fusion | flops 11796560 | bytes 3670176 | tf_op jit(solution)/shard_map/pi,vciw->pvcw/dot_general | solution.py:82
  89.2 10.5 %fusion.21 = f32[10,64,2048]{2,1,0:T(8,128)} fusion(bf16[10,128,2048]{2,1,0:T(8,128)(2,1)} %param.12, bf16[10,128,2048]{2,1,0:T(8,128)(2,1)} %param.13, bf16[10,64,2048]{2,0,1:T(8,128)(2,1)} %convolution_convert_fusion, f32[10,128]{1,0:T(8,128)S(1)} %fusion.34), kind=kOutput, calls=%fused_computation.14 | convolution fusion | flops 671252480 | bytes 18355200 | tf_op jit(solution)/shard_map/pvk,pkn->pvn/dot_general | solution.py:88
  99.6 14.7 %fusion = f32[64,2048,4]{1,2,0:T(4,128)S(1)} fusion(f32[10,64,2048]{2,1,0:T(8,128)} %fusion.21, s32[10,4]{0,1:T(4,128)S(1)} %get-tuple-element.3), kind=kOutput, calls=%fused_computation | convolution fusion | flops 62914600 | bytes 7340192 | tf_op jit(solution)/shard_map/pb,pvn->vbn/dot_general | solution.py:89
  114.4 2.6 %copy.27 = f32[8,8,4,2048]{3,1,2,0:T(8,128)} copy(f32[8,8,4,2048]{3,2,1,0:T(4,128)S(1)} %bitcast.39) | data formatting | bytes 4194304
  116.9 0.0 reduce-scatter.5.cloned.1.call-update
  116.9 0.0 all-reduce.2.cloned.1.call-done
  117.0 61.8 %reduce-scatter.3.cloned.1.call-done = f32[1,64,512]{2,1,0:T(8,128)} async-done(((f32[16,64,512]{2,1,0:T(8,128)}), f32[1,64,512]{2,1,0:T(8,128)}) %reduce-scatter.3.cloned.1.call-update) | async-done | bytes 131088 | tf_op jit(solution)/shard_map/reduce_scatter | solution.py:69
  178.7 0.0 copy-done
  178.7 2.4 %fusion.29 = bf16[64,512]{1,0:T(8,128)(2,1)} fusion(bf16[64,2048]{1,0:T(8,128)(2,1)} %all-reduce.2.cloned.1.call-done, bf16[512,2048]{1,0:T(8,128)(2,1)S(1)} %copy-done, f32[1,64,512]{2,1,0:T(8,128)} %reduce-scatter.3.cloned.1.call-done), kind=kOutput, calls=%fused_computation.18 | convolution fusion | flops 134283264 | bytes 2555904 | tf_op jit(solution)/shard_map/vn,wn->vw/dot_general | solution.py:77
  181.1 42.6 %reduce-scatter.5.cloned.1.call-done = f32[64,2048]{1,0:T(8,128)} async-done(((f32[64,8192]{1,0:T(8,128)}), f32[64,2048]{1,0:T(8,128)}) %reduce-scatter.5.cloned.1.call-update) | async-done | bytes 524304 | tf_op jit(solution)/shard_map/reduce_scatter | solution.py:91
  223.7 1.8 convert_element_type.63
  (6 shorter events, 0.1 us)
Async XLA Ops:
  7.2 171.6 %copy-start = (bf16[512,2048]{1,0:T(8,128)(2,1)S(1)}, bf16[512,2048]{1,0:T(8,128)(2,1)}, u32[]{:S(2)}) copy-start(bf16[512,2048]{1,0:T(8,128)(2,1)} %param.9) | copy-start | bytes 6291460
  7.2 33.1 %all-gather.3.cloned.1.call-start = ((), (), s32[]{:S(2)}) async-start(), calls=%async_computation.2 | async-start | bytes 1310720 | tf_op jit(solution)/shard_map/all_gather | solution.py:55
  7.9 73.1 %all-gather.5.cloned.1.call-start = ((), (), s32[]{:S(2)}) async-start(), calls=%async_computation.5 | async-start | bytes 1114112 | tf_op jit(solution)/shard_map/all_gather | solution.py:80
  8.7 108.3 %all-reduce.2.cloned.1.call-start = ((), (), s32[]{:S(2)}) async-start(), calls=%async_computation.4 | async-start | bytes 524288 | tf_op jit(solution)/shard_map/psum | solution.py:11
  64.9 113.9 %reduce-scatter.3.cloned.1.call-start = ((), (), s32[]{:S(2)}) async-start(), calls=%async_computation.3 | async-start | bytes 2228224 | tf_op jit(solution)/shard_map/reduce_scatter | solution.py:69
  80.7 143.0 %reduce-scatter.5.cloned.1.call-start = ((), (), s32[]{:S(2)}) async-start(), calls=%async_computation.6 | async-start | bytes 2621440 | tf_op jit(solution)/shard_map/reduce_scatter | solution.py:91
Sparse Core Ops, SparseCore 0:
  9.6 30.6 all-gather.2
  42.3 36.2 all-gather.4
  81.6 31.4 all-reduce.1
  117.1 61.5 reduce-scatter.2
  180.9 42.8 reduce-scatter.4
where the time goes:
time: 232 us
  waiting for transfers between devices  134 us (58%)
  matrix products  57.2 us (25%)
  local copies, waits for them, and re-layouts  20.5 us (9%)
  between operations  13.9 us (6%)
  other arithmetic  5.79 us (2%)
    reduce_scatter x1, waiting for transfers between devices, body(): lax.psum_scatter(partial_value.reshape(col_count * row_count, vec_count,...  61.8 us
    reduce_scatter x1, waiting for transfers between devices, body(): lax.psum_scatter(column_part, 'row', scatter_dimension=1, tiled=True)  42.6 us
    all_gather x1, waiting for transfers between devices, body(): gathered_x = lax.all_gather(right_vectors, 'row', axis=1, tiled=True)  28.2 us
    dot_general x1, matrix products, body(): jnp.einsum('pb,pvn->vbn', col_hot, returned, precision=highest)  14.7 us
    dot_general x1, matrix products, body(): jnp.einsum('pi,pvcw->civw', row_hot, products, precision=highest)  13.1 us
    dot_general x1, matrix products, body(): jnp.einsum('pvk,pkn->pvn', coefficients, u_panels, preferred_element_type...  10.5 us
    dot_general x1, matrix products, body(): jnp.einsum('pvk,pkn->pvn', transposed, v_panels, preferred_element_type=j...  10.5 us
    reshape x1, local copies, waits for them, and re-layouts, body(): products = products.reshape(slot_count, vec_count, col_count, sub_width)  7.56 us
  transfers between devices with their start and end apart: 5, of which 3 were waited for; matrix products, arithmetic and copies ran while one was open for 35% of the time, Pallas kernels for 0%

commit v1 on v0

v1 whole, which is shorter than its diff:
```python
import functools

import jax
import jax.numpy as jnp
from jax import lax
from jax.experimental import pallas as pl
from jax.experimental.pallas import tpu as pltpu
from jax.sharding import PartitionSpec as P

PANEL = 128
MESH = pl.DeviceIdType.MESH


def dot_nt(a, b):
    return lax.dot_general(a, b, (((1,), (1,)), ((), ())), preferred_element_type=jnp.float32)


def kernel(
    dims, ranks, order, x_hbm, w_hbm, diag_hbm, v_hbm, u_hbm, rows_out, cols_out,
    xg, wg, dvec, diag, v, u, row_ids, col_ids, lhs_rows, lhs_cols, p_rows, p_cols, sum3,
    col_sr, col_rr, col_sl, col_rl, s1, r1, s2, r2, s3, r3,
    load_sem, w_zr, w_zl, w_x, w_c, x_zr, x_zl, d_sem, c_zr, c_zl, r1_sem, r2_sem, r3_sem,
):
    R, C, V, W, Q, TILE, PG = dims
    X = C // 2
    total = v.shape[0]
    slots = total // PANEL
    grp, c, z = lax.axis_index("groups"), lax.axis_index("col"), lax.axis_index("row")
    mx, core = c // 2, c % 2
    sib = mx * 2 + (1 - core)
    row_of = lambda zz: (grp, c, zz)
    col_of = lambda cc: (grp, cc, z)
    sends = []

    def when(cond, fn):
        if cond is True:
            fn()
        else:
            pl.when(cond)(fn)

    def send(cond, make):
        when(cond, lambda: make().start())
        sends.append((cond, make))

    def rows_at(i):
        return pl.ds(pl.multiple_of(i * V, V), V)

    def lanes_at(i, n):
        return pl.ds(pl.multiple_of(i * n, n), n)

    def remote(src, dst, sems, dev):
        return pltpu.make_async_remote_copy(
            src_ref=src, dst_ref=dst, send_sem=sems[0], recv_sem=sems[1],
            device_id=dev, device_id_type=MESH,
        )

    def pair(sem, *index):
        return sem.at[(0, *index)], sem.at[(1, *index)]

    def x_slot(ref, r):
        return ref.at[rows_at(r * W // TILE), lanes_at(r % (TILE // W), W)]

    def w_slot(i, cc):
        return wg.at[rows_at(i), lanes_at(cc, Q)]

    load_x = pltpu.make_async_copy(x_hbm, x_slot(xg, z), load_sem.at[0])
    load_w = pltpu.make_async_copy(w_hbm, w_slot(z, c), load_sem.at[1])
    load_u = pltpu.make_async_copy(u_hbm, u, load_sem.at[2])
    load_v = pltpu.make_async_copy(v_hbm, v, load_sem.at[3])
    load_d = pltpu.make_async_copy(diag_hbm, diag, load_sem.at[4])
    for load in (load_w, load_x, load_u, load_v, load_d):
        load.start()

    barrier = pltpu.get_barrier_semaphore()
    for step in range(1, R):
        pl.semaphore_signal(barrier, inc=1, device_id=row_of((z + step) % R), device_id_type=MESH)
    for step in range(1, C):
        pl.semaphore_signal(barrier, inc=1, device_id=col_of((c + step) % C), device_id_type=MESH)
    pl.semaphore_wait(barrier, R + C - 2)

    def w_right(s):
        return remote(w_slot(z - s, c), w_slot(z - s, c), pair(w_zr, s), row_of(z + 1))

    def w_left(s):
        return remote(w_slot(z + s, c), w_slot(z + s, c), pair(w_zl, s), row_of(z - 1))

    def w_across(i, dx):
        return remote(w_slot(i, c), w_slot(i, c), pair(w_x, dx, i), col_of((mx + dx) % X * 2 + core))

    def w_sibling(i, dx):
        cc = (mx + dx) % X * 2 + core
        return remote(w_slot(i, cc), w_slot(i, cc), pair(w_c, dx, i), col_of(sib))

    def w_spread(cond, i):
        for dx in range(1, X):
            send(cond, lambda dx=dx: w_across(i, dx))
        send(cond, lambda: w_sibling(i, 0))

    def w_crossed(cond, i):
        for dx in range(1, X):
            cc = (mx - dx + X) % X * 2 + core
            arrived = lambda dx=dx, cc=cc: remote(
                w_slot(i, cc), w_slot(i, cc), pair(w_x, dx, i), col_of(c)).wait_recv()
            when(cond, arrived)
            send(cond, lambda dx=dx: w_sibling(i, X - dx))

    def x_right(s):
        return remote(x_slot(xg, z - s), x_slot(xg, z - s), pair(x_zr, s), row_of(z + 1))

    def x_left(s):
        return remote(x_slot(xg, z + s), x_slot(xg, z + s), pair(x_zl, s), row_of(z - 1))

    def x_send(s):
        send((z < R - 1) & (z >= s), lambda: x_right(s))
        send((z > 0) & (z + s < R), lambda: x_left(s))

    def x_wait(s):
        pl.when(z - 1 - s >= 0)(lambda: remote(
            x_slot(xg, z - 1 - s), x_slot(xg, z - 1 - s), pair(x_zr, s), row_of(z)).wait_recv())
        pl.when(z + 1 + s < R)(lambda: remote(
            x_slot(xg, z + 1 + s), x_slot(xg, z + 1 + s), pair(x_zl, s), row_of(z)).wait_recv())

    load_w.wait()
    send(z < R - 1, lambda: w_right(0))
    send(z > 0, lambda: w_left(0))
    w_spread(True, z)
    load_x.wait()
    x_send(0)

    lane = lax.broadcasted_iota(jnp.int32, (1, total), 1) + z * total
    in_row = jnp.full((1, total), -1, jnp.int32)
    in_col = jnp.full((1, total), -1, jnp.int32)
    start = jnp.int32(0)
    for p in range(R * PG):
        tile = order[0, p]
        ti, tj = tile // PG, tile % PG
        rank = jnp.where(ti == c * PG + tj, 0, ranks[ti, tj])
        offset = lane - start * PANEL
        hit = (offset >= 0) & (offset < rank)
        in_row = jnp.where(hit, ti, in_row)
        in_col = jnp.where(hit, tj, in_col)
        start = start + (rank + PANEL - 1) // PANEL
    row_ids[...] = in_row
    col_ids[...] = in_col

    for s in range(R - 1):
        from_left, from_right = z - 1 - s, z + 1 + s
        pl.when(from_left >= 0)(lambda: remote(
            w_slot(from_left, c), w_slot(from_left, c), pair(w_zr, s), row_of(z)).wait_recv())
        if s < R - 2:
            send((z < R - 1) & (from_left >= 0), lambda s=s: w_right(s + 1))
        w_spread(from_left >= 0, from_left)
        pl.when(from_right < R)(lambda: remote(
            w_slot(from_right, c), w_slot(from_right, c), pair(w_zl, s), row_of(z)).wait_recv())
        if s < R - 2:
            send((z > 0) & (from_right < R), lambda s=s: w_left(s + 1))
        w_spread(from_right < R, from_right)
        if s == 0:
            w_crossed(True, z)
        else:
            w_crossed(z - s >= 0, z - s)
            w_crossed(z + s < R, z + s)
    w_crossed(z - (R - 1) >= 0, z - (R - 1))
    w_crossed(z + (R - 1) < R, z + (R - 1))

    x_wait(0)
    if R > 2:
        x_send(1)

    root = z // PG
    diag_early = W == TILE and R <= PG

    def diag_send():
        for step in range(1, C):
            send(c == root, lambda step=step: remote(
                xg.at[rows_at(z % PG)], dvec, pair(d_sem, step), col_of((c + step) % C)))

    if diag_early:
        diag_send()

    for dx in range(X):
        cc = (mx + dx) % X * 2 + (1 - core)
        for i in range(R):
            remote(w_slot(i, cc), w_slot(i, cc), pair(w_c, dx, i), col_of(c)).wait_recv()

    def project(src, count, panels, ids, other_ids, lhs, other_count):
        width = 256 if total % 256 == 0 else PANEL

        def step(k, carry):
            lanes = lanes_at(k, width)
            res = dot_nt(src[...], panels[lanes, :])
            own, other = ids[:, lanes], other_ids[:, lanes]
            found = jnp.zeros((V, width), jnp.float32)
            for i in range(count):
                found = jnp.where(own == i, res[i * V:(i + 1) * V], found)
            for j in range(other_count):
                lhs[j * V:(j + 1) * V, lanes] = jnp.where(other == j, found, 0.0).astype(lhs.dtype)
            return carry

        lax.fori_loop(0, total // width, step, 0)

    def expand(lhs, panels, out):
        width = min(256, TILE)

        def step(k, carry):
            lanes = lanes_at(k, width)
            out[:, lanes] = jnp.dot(lhs[...], panels[:, lanes], preferred_element_type=jnp.float32)
            return carry

        lax.fori_loop(0, TILE // width, step, 0)

    load_u.wait()
    project(wg, R, u, row_ids, col_ids, lhs_cols, PG)
    load_v.wait()
    expand(lhs_cols, v, p_cols)

    def col_part(d):
        return p_cols[rows_at(d * W // TILE), lanes_at(d % (TILE // W), W)]

    def col_phase(k):
        t_right, t_left = k - z, k - (R - 1 - z)
        go_right, go_left = (z <= k) & (z < R - 1), (R - 1 - z <= k) & (z > 0)

        def right():
            return remote(col_sr.at[t_right], col_rr.at[t_right], pair(c_zr, t_right), row_of(z + 1))

        def left():
            return remote(col_sl.at[t_left], col_rl.at[t_left], pair(c_zl, t_left), row_of(z - 1))

        @pl.when(go_right & (z == 0))
        def _():
            col_sr[t_right] = col_part(R - 1 - t_right).astype(col_sr.dtype)

        @pl.when(go_right & (z > 0))
        def _():
            remote(col_sr.at[t_right], col_rr.at[t_right], pair(c_zr, t_right), row_of(z)).wait_recv()
            col_sr[t_right] = (col_part(R - 1 - t_right) + col_rr[t_right].astype(jnp.float32)).astype(col_sr.dtype)

        send(go_right, right)

        @pl.when(go_left & (z == R - 1))
        def _():
            col_sl[t_left] = col_part(t_left).astype(col_sl.dtype)

        @pl.when(go_left & (z < R - 1))
        def _():
            remote(col_sl.at[t_left], col_rl.at[t_left], pair(c_zl, t_left), row_of(z)).wait_recv()
            col_sl[t_left] = (col_part(t_left) + col_rl[t_left].astype(jnp.float32)).astype(col_sl.dtype)

        send(go_left, left)

    for k in range(R - 2):
        col_phase(k)
        x_wait(k + 1)
        if k + 2 < R - 1:
            x_send(k + 2)
    if R == 2:
        pass
    if not diag_early:
        diag_send()

    project(xg, PG, v, col_ids, row_ids, lhs_rows, R)
    expand(lhs_rows, u, p_rows)

    for dx in range(X):
        xx = (mx + dx) % X
        s1[dx] = p_rows[:, lanes_at(xx * 2 + 1 - core, Q)].astype(s1.dtype)
        send(True, lambda dx=dx: remote(s1.at[dx], r1.at[dx], pair(r1_sem, dx), col_of(sib)))

    col_phase(R - 2)

    for dx in list(range(1, X)) + [0]:
        remote(s1.at[dx], r1.at[dx], pair(r1_sem, dx), col_of(c)).wait_recv()
        xx = (mx + dx) % X
        part = p_rows[:, lanes_at(xx * 2 + core, Q)] + r1[dx].astype(jnp.float32)
        if dx:
            s2[dx] = part.astype(s2.dtype)
            send(True, lambda dx=dx, xx=xx: remote(
                s2.at[dx], r2.at[dx], pair(r2_sem, dx), col_of(xx * 2 + core)))
        else:
            sum3[...] = part

    load_d.wait()
    pl.when(c == root)(lambda: dvec.__setitem__(..., xg[rows_at(z % PG)]))
    for step in range(1, C):
        pl.when((c != root) & (c == (root + step) % C))(lambda step=step: remote(
            dvec, dvec, pair(d_sem, step), col_of(c)).wait_recv())
    diag_part = dot_nt(dvec[...], diag[...])

    for dx in range(1, X):
        remote(s2.at[dx], r2.at[dx], pair(r2_sem, dx), col_of(c)).wait_recv()
        sum3[...] += r2[dx].astype(jnp.float32)
    s3[...] = sum3[...].astype(s3.dtype)
    for step in range(1, R):
        to = (z + step) % R
        send(True, lambda step=step, to=to: remote(
            s3.at[rows_at(to)], r3.at[rows_at(step)], pair(r3_sem, step), row_of(to)))

    result = col_part(z)
    cols_out[...] = result.astype(cols_out.dtype)
    acc = p_cols.at[rows_at(z * W // TILE), lanes_at(z % (TILE // W), W)]

    @pl.when(z > 0)
    def _():
        t = R - 1 - z
        remote(col_sr.at[t], col_rr.at[t], pair(c_zr, t), row_of(z)).wait_recv()
        acc[...] += col_rr[t].astype(jnp.float32)

    @pl.when(z < R - 1)
    def _():
        remote(col_sl.at[z], col_rl.at[z], pair(c_zl, z), row_of(z)).wait_recv()
        acc[...] += col_rl[z].astype(jnp.float32)

    cols_out[...] = acc[...].astype(cols_out.dtype)

    out = sum3[rows_at(z)] + diag_part
    for step in range(1, R):
        remote(s3.at[rows_at(0)], r3.at[rows_at(step)], pair(r3_sem, step), row_of(z)).wait_recv()
        out = out + r3[rows_at(step)].astype(jnp.float32)
    rows_out[...] = out.astype(rows_out.dtype)

    for cond, make in sends:
        when(cond, lambda make=make: make().wait_send())


def body(mesh_shape, right_vectors, left_vectors, diag_tiles, tile_ranks, tile_order, v_panels, u_panels):
    R, C = mesh_shape["row"], mesh_shape["col"]
    X = C // 2
    V, W = right_vectors.shape
    Q = left_vectors.shape[1]
    TILE = diag_tiles.shape[1]
    PG = tile_ranks.shape[1]
    total = v_panels.shape[0] * PANEL
    b16, f32 = jnp.bfloat16, jnp.float32
    any_spec = pl.BlockSpec(memory_space=pl.ANY)
    smem = pl.BlockSpec(memory_space=pltpu.SMEM)
    vmem = pl.BlockSpec(memory_space=pltpu.VMEM)
    dma = pltpu.SemaphoreType.DMA
    steps = R - 1
    return pl.pallas_call(
        functools.partial(kernel, (R, C, V, W, Q, TILE, PG)),
        out_shape=(
            jax.ShapeDtypeStruct((V, Q), b16),
            jax.ShapeDtypeStruct((V, W), b16),
        ),
        in_specs=[smem, smem] + [any_spec] * 5,
        out_specs=(vmem, vmem),
        scratch_shapes=[
            pltpu.VMEM((PG * V, TILE), b16),
            pltpu.VMEM((R * V, TILE), b16),
            pltpu.VMEM((V, TILE), b16),
            pltpu.VMEM((Q, TILE), b16),
            pltpu.VMEM((total, TILE), b16),
            pltpu.VMEM((total, TILE), b16),
            pltpu.VMEM((1, total), jnp.int32),
            pltpu.VMEM((1, total), jnp.int32),
            pltpu.VMEM((R * V, total), b16),
            pltpu.VMEM((PG * V, total), b16),
            pltpu.VMEM((R * V, TILE), f32),
            pltpu.VMEM((PG * V, TILE), f32),
            pltpu.VMEM((R * V, Q), f32),
            pltpu.VMEM((steps, V, W), b16),
            pltpu.VMEM((steps, V, W), b16),
            pltpu.VMEM((steps, V, W), b16),
            pltpu.VMEM((steps, V, W), b16),
            pltpu.VMEM((X, R * V, Q), b16),
            pltpu.VMEM((X, R * V, Q), b16),
            pltpu.VMEM((X, R * V, Q), b16),
            pltpu.VMEM((X, R * V, Q), b16),
            pltpu.VMEM((R * V, Q), b16),
            pltpu.VMEM((R * V, Q), b16),
            dma((5,)),
            dma((2, steps)),
            dma((2, steps)),
            dma((2, X, R)),
            dma((2, X, R)),
            dma((2, steps)),
            dma((2, steps)),
            dma((2, C)),
            dma((2, steps)),
            dma((2, steps)),
            dma((2, X)),
            dma((2, X)),
            dma((2, R)),
        ],
        compiler_params=pltpu.CompilerParams(
            collective_id=0, has_side_effects=True, vmem_limit_bytes=48 * 1024 * 1024
        ),
        name="slab",
    )(
        tile_ranks, tile_order, right_vectors, left_vectors, diag_tiles,
        v_panels.reshape(total, TILE), u_panels.reshape(total, TILE),
    )


def solution(mesh):
    in_specs = (
        P("groups", ("col", "row")),
        P("groups", ("row", "col")),
        P(("groups", "row", "col"), None),
        P("groups", "col"),
        P(("groups", "col"), None),
        P(("groups", "col", "row"), None, None),
        P(("groups", "col", "row"), None, None),
    )
    out_specs = (P("groups", ("row", "col")), P("groups", ("col", "row")))
    return jax.shard_map(
        functools.partial(body, dict(mesh.shape)),
        mesh=mesh, in_specs=in_specs, out_specs=out_specs, check_vma=False,
    )
```

time: 232 us -> 63.7 us (0.27)
  waiting for transfers between devices: 134 us -> 0 us
  matrix products: 57.2 us -> 0 us
  Pallas kernels: 0 us -> 56.8 us
  local copies, waits for them, and re-layouts: 20.5 us -> 6.04 us
  between operations: 13.9 us -> 0.65 us
  other arithmetic: 5.79 us -> 0 us
    reduce_scatter x2 -> x0, waiting for transfers between devices: 104 us -> none  [the longest x1 61.8 us: body(): lax.psum_scatter(partial_value.reshape(col_count * row_count, vec_count,...]
    dot_general x7 -> x0, matrix products: 57.2 us -> none  [the longest x1 14.7 us: body(): jnp.einsum('pb,pvn->vbn', col_hot, returned, precision=highest)]
    pallas_call x0 -> x1, Pallas kernels: none -> 56.8 us  [body(): pl.pallas_call(functools.partial(kernel, (R, C, V, W, Q, TILE, PG)), out_...]
    all_gather x2 -> x0, waiting for transfers between devices: 28.2 us -> none  [the longest x1 28.2 us: body(): gathered_x = lax.all_gather(right_vectors, 'row', axis=1, tiled=True)]
    reshape x6 -> x0, local copies, waits for them, and re-layouts: 15.9 us -> none  [the longest x1 7.56 us: body(): products = products.reshape(slot_count, vec_count, col_count, sub_width)]
    unnamed x3 -> x12, local copies, waits for them, and re-layouts: 2.56 us -> 6.04 us
    convert_element_type x4 -> x0, other arithmetic: 2.64 us -> none  [the longest x1 1.77 us: body(): lax.psum_scatter(column_part, 'row', scatter_dimension=1, tiled=True)]
  transfers between devices with their start and end apart: 5 -> 0, of which waited for: 3 -> 0; matrix products, arithmetic and copies ran while one was open for 35% -> 0% of each run, Pallas kernels for 0% -> 0%
where the time goes in v1:
time: 63.7 us; the launch traced here: 63.4 us
  Pallas kernels  56.8 us (89%)
  local copies, waits for them, and re-layouts  6.04 us (9%)
  between operations  0.65 us (1%)
    pallas_call x1, Pallas kernels, body(): pl.pallas_call(functools.partial(kernel, (R, C, V, W, Q, TILE, PG)), out_...  56.8 us
    unnamed x12, local copies, waits for them, and re-layouts  6.04 us

profile of v1, /device:TPU:0, one launch (start us, length us, event | category | flops | bytes accessed | tf_op | source)
XLA Modules:
  0.0 63.4 jit_solution(11711436842104694495)
XLA Ops:
  0.6 0.0 copy-start
  0.6 1.6 %copy-done = bf16[512,2048]{1,0:T(8,128)(2,1)S(1)} copy-done((bf16[512,2048]{1,0:T(8,128)(2,1)S(1)}, bf16[512,2048]{1,0:T(8,128)(2,1)}, u32[]{:S(2)}) %copy-start) | copy-done | bytes 2097176
  2.2 0.0 copy-start.1
  2.2 0.9 %copy-done.1 = bf16[64,2048]{1,0:T(8,128)(2,1)S(1)} copy-done((bf16[64,2048]{1,0:T(8,128)(2,1)S(1)}, bf16[64,2048]{1,0:T(8,128)(2,1)}, u32[]{:S(2)}) %copy-start.1) | copy-done | bytes 262168
  3.2 0.0 copy-start.2
  3.2 0.8 %copy-done.2 = bf16[64,512]{1,0:T(8,128)(2,1)S(1)} copy-done((bf16[64,512]{1,0:T(8,128)(2,1)S(1)}, bf16[64,512]{1,0:T(8,128)(2,1)}, u32[]{:S(2)}) %copy-start.2) | copy-done | bytes 65560
  4.0 0.0 copy-start.3
  4.0 0.7 %copy-done.3 = s32[4,4]{1,0:T(4,128)S(1)} copy-done((s32[4,4]{1,0:T(4,128)S(1)}, s32[4,4]{1,0:T(4,128)}, u32[]{:S(2)}) %copy-start.3) | copy-done | bytes 88
  4.7 0.0 copy-start.4
  4.7 0.7 %copy-done.4 = s32[1,16]{1,0:T(1,128)S(1)} copy-done((s32[1,16]{1,0:T(1,128)S(1)}, s32[1,16]{1,0:T(1,128)}, u32[]{:S(2)}) %copy-start.4) | copy-done | bytes 88
  5.4 56.8 %slab.1 = (bf16[64,512]{1,0:T(8,128)(2,1)S(1)}, bf16[64,2048]{1,0:T(8,128)(2,1)S(1)}) custom-call(s32[4,4]{1,0:T(4,128)S(1)} %copy-done.3, s32[1,16]{1,0:T(1,128)S(1)} %copy-done.4, bf16[64,2048]{1,0:T(8,128)(2,1)S(1)} %copy-done.1, bf16[64,512]{1,0:T(8,128)(2,1)S(1)} %copy-done.2, bf16[512,2048]{1,0:T(8,128)(2,1)S(1)} %copy-done, ...), custom_call_target="tpu_custom_call" | custom-call | tf_op jit(solution)/shard_map/slab/pallas_call | solution.py:340
  62.1 0.6 copy.11
  62.7 0.7 %copy.12 = bf16[64,2048]{1,0:T(8,128)(2,1)} copy(bf16[64,2048]{1,0:T(8,128)(2,1)S(1)} %get-tuple-element.5) | data formatting | bytes 524288
Async XLA Ops:
  0.6 1.6 %copy-start = (bf16[512,2048]{1,0:T(8,128)(2,1)S(1)}, bf16[512,2048]{1,0:T(8,128)(2,1)}, u32[]{:S(2)}) copy-start(bf16[512,2048]{1,0:T(8,128)(2,1)} %diag_hbm.1) | copy-start | bytes 6291460
  2.2 0.9 %copy-start.1 = (bf16[64,2048]{1,0:T(8,128)(2,1)S(1)}, bf16[64,2048]{1,0:T(8,128)(2,1)}, u32[]{:S(2)}) copy-start(bf16[64,2048]{1,0:T(8,128)(2,1)} %x_hbm.1) | copy-start | bytes 786436
  3.2 0.8 %copy-start.2 = (bf16[64,512]{1,0:T(8,128)(2,1)S(1)}, bf16[64,512]{1,0:T(8,128)(2,1)}, u32[]{:S(2)}) copy-start(bf16[64,512]{1,0:T(8,128)(2,1)} %w_hbm.1) | copy-start | bytes 196612
  4.0 0.7 %copy-start.3 = (s32[4,4]{1,0:T(4,128)S(1)}, s32[4,4]{1,0:T(4,128)}, u32[]{:S(2)}) copy-start(s32[4,4]{1,0:T(4,128)} %ranks.1) | copy-start | bytes 196
  4.7 0.7 %copy-start.4 = (s32[1,16]{1,0:T(1,128)S(1)}, s32[1,16]{1,0:T(1,128)}, u32[]{:S(2)}) copy-start(s32[1,16]{1,0:T(1,128)} %order.1) | copy-start | bytes 196

commit v2 on v1

--- a/solution.py
+++ b/solution.py
@@ -8,6 +8,7 @@
 from jax.sharding import PartitionSpec as P
 
 PANEL = 128
+HALVES = 2
 MESH = pl.DeviceIdType.MESH
 
 
@@ -24,7 +25,7 @@
     R, C, V, W, Q, TILE, PG = dims
     X = C // 2
     total = v.shape[0]
-    slots = total // PANEL
+    H = V // HALVES
     grp, c, z = lax.axis_index("groups"), lax.axis_index("col"), lax.axis_index("row")
     mx, core = c // 2, c % 2
     sib = mx * 2 + (1 - core)
@@ -57,8 +58,11 @@
     def pair(sem, *index):
         return sem.at[(0, *index)], sem.at[(1, *index)]
 
-    def x_slot(ref, r):
-        return ref.at[rows_at(r * W // TILE), lanes_at(r % (TILE // W), W)]
+    def x_slot(ref, r, h=None):
+        lanes = lanes_at(r % (TILE // W), W)
+        if h is None:
+            return ref.at[rows_at(r * W // TILE), lanes]
+        return ref.at[pl.ds(pl.multiple_of(r * W // TILE * V + h * H, H), H), lanes]
 
     def w_slot(i, cc):
         return wg.at[rows_at(i), lanes_at(cc, Q)]
@@ -79,10 +83,10 @@
     pl.semaphore_wait(barrier, R + C - 2)
 
     def w_right(s):
-        return remote(w_slot(z - s, c), w_slot(z - s, c), pair(w_zr, s), row_of(z + 1))
+        return remote(w_slot(z, c), w_slot(z, c), pair(w_zr, s), row_of(z + 1 + s))
 
     def w_left(s):
-        return remote(w_slot(z + s, c), w_slot(z + s, c), pair(w_zl, s), row_of(z - 1))
+        return remote(w_slot(z, c), w_slot(z, c), pair(w_zl, s), row_of(z - 1 - s))
 
     def w_across(i, dx):
         return remote(w_slot(i, c), w_slot(i, c), pair(w_x, dx, i), col_of((mx + dx) % X * 2 + core))
@@ -104,28 +108,40 @@
             when(cond, arrived)
             send(cond, lambda dx=dx: w_sibling(i, X - dx))
 
-    def x_right(s):
-        return remote(x_slot(xg, z - s), x_slot(xg, z - s), pair(x_zr, s), row_of(z + 1))
-
-    def x_left(s):
-        return remote(x_slot(xg, z + s), x_slot(xg, z + s), pair(x_zl, s), row_of(z - 1))
-
-    def x_send(s):
-        send((z < R - 1) & (z >= s), lambda: x_right(s))
-        send((z > 0) & (z + s < R), lambda: x_left(s))
-
-    def x_wait(s):
-        pl.when(z - 1 - s >= 0)(lambda: remote(
-            x_slot(xg, z - 1 - s), x_slot(xg, z - 1 - s), pair(x_zr, s), row_of(z)).wait_recv())
-        pl.when(z + 1 + s < R)(lambda: remote(
-            x_slot(xg, z + 1 + s), x_slot(xg, z + 1 + s), pair(x_zl, s), row_of(z)).wait_recv())
+    def x_half(r, h):
+        return x_slot(xg, r, h)
+
+    def x_right(s, h):
+        return remote(x_half(z - s, h), x_half(z - s, h), pair(x_zr, s, h), row_of(z + 1))
+
+    def x_left(s, h):
+        return remote(x_half(z + s, h), x_half(z + s, h), pair(x_zl, s, h), row_of(z - 1))
+
+    def x_send(s, h):
+        send((z < R - 1) & (z >= s), lambda: x_right(s, h))
+        send((z > 0) & (z + s < R), lambda: x_left(s, h))
+
+    def x_wait(s, h):
+        left, right = z - 1 - s, z + 1 + s
+        pl.when(left >= 0)(lambda: remote(
+            x_half(left, h), x_half(left, h), pair(x_zr, s, h), row_of(z)).wait_recv())
+        pl.when(right < R)(lambda: remote(
+            x_half(right, h), x_half(right, h), pair(x_zl, s, h), row_of(z)).wait_recv())
+
+    def x_pass(s):
+        for h in range(HALVES):
+            x_wait(s, h)
+            if s + 1 < R - 1:
+                x_send(s + 1, h)
 
     load_w.wait()
-    send(z < R - 1, lambda: w_right(0))
-    send(z > 0, lambda: w_left(0))
+    for s in range(R - 1):
+        send(z + 1 + s < R, lambda s=s: w_right(s))
+        send(z - 1 - s >= 0, lambda s=s: w_left(s))
     w_spread(True, z)
     load_x.wait()
-    x_send(0)
+    for h in range(HALVES):
+        x_send(0, h)
 
     lane = lax.broadcasted_iota(jnp.int32, (1, total), 1) + z * total
     in_row = jnp.full((1, total), -1, jnp.int32)
@@ -147,13 +163,9 @@
         from_left, from_right = z - 1 - s, z + 1 + s
         pl.when(from_left >= 0)(lambda: remote(
             w_slot(from_left, c), w_slot(from_left, c), pair(w_zr, s), row_of(z)).wait_recv())
-        if s < R - 2:
-            send((z < R - 1) & (from_left >= 0), lambda s=s: w_right(s + 1))
         w_spread(from_left >= 0, from_left)
         pl.when(from_right < R)(lambda: remote(
             w_slot(from_right, c), w_slot(from_right, c), pair(w_zl, s), row_of(z)).wait_recv())
-        if s < R - 2:
-            send((z > 0) & (from_right < R), lambda s=s: w_left(s + 1))
         w_spread(from_right < R, from_right)
         if s == 0:
             w_crossed(True, z)
@@ -163,9 +175,7 @@
     w_crossed(z - (R - 1) >= 0, z - (R - 1))
     w_crossed(z + (R - 1) < R, z + (R - 1))
 
-    x_wait(0)
-    if R > 2:
-        x_send(1)
+    x_pass(0)
 
     root = z // PG
     diag_early = W == TILE and R <= PG
@@ -199,86 +209,97 @@
 
         lax.fori_loop(0, total // width, step, 0)
 
-    def expand(lhs, panels, out):
-        width = min(256, TILE)
+    def expand(lhs, panels, out, first, count):
+        width = min(256, count)
 
         def step(k, carry):
-            lanes = lanes_at(k, width)
+            lanes = pl.ds(pl.multiple_of(first + k * width, width), width)
             out[:, lanes] = jnp.dot(lhs[...], panels[:, lanes], preferred_element_type=jnp.float32)
             return carry
 
-        lax.fori_loop(0, TILE // width, step, 0)
+        lax.fori_loop(0, count // width, step, 0)
 
     load_u.wait()
+    if R > 2:
+        x_pass(1)
     project(wg, R, u, row_ids, col_ids, lhs_cols, PG)
     load_v.wait()
-    expand(lhs_cols, v, p_cols)
-
-    def col_part(d):
-        return p_cols[rows_at(d * W // TILE), lanes_at(d % (TILE // W), W)]
-
-    def col_phase(k):
+    expand(lhs_cols, v, p_cols, 0, TILE)
+
+    def col_slot(d, h=None):
+        lanes = lanes_at(d % (TILE // W), W)
+        if h is None:
+            return p_cols.at[rows_at(d * W // TILE), lanes]
+        return p_cols.at[pl.ds(pl.multiple_of(d * W // TILE * V + h * H, H), H), lanes]
+
+    def col_phase(k, h):
         t_right, t_left = k - z, k - (R - 1 - z)
         go_right, go_left = (z <= k) & (z < R - 1), (R - 1 - z <= k) & (z > 0)
-
-        def right():
-            return remote(col_sr.at[t_right], col_rr.at[t_right], pair(c_zr, t_right), row_of(z + 1))
-
-        def left():
-            return remote(col_sl.at[t_left], col_rl.at[t_left], pair(c_zl, t_left), row_of(z - 1))
-
-        @pl.when(go_right & (z == 0))
-        def _():
-            col_sr[t_right] = col_part(R - 1 - t_right).astype(col_sr.dtype)
-
-        @pl.when(go_right & (z > 0))
-        def _():
-            remote(col_sr.at[t_right], col_rr.at[t_right], pair(c_zr, t_right), row_of(z)).wait_recv()
-            col_sr[t_right] = (col_part(R - 1 - t_right) + col_rr[t_right].astype(jnp.float32)).astype(col_sr.dtype)
-
-        send(go_right, right)
-
-        @pl.when(go_left & (z == R - 1))
-        def _():
-            col_sl[t_left] = col_part(t_left).astype(col_sl.dtype)
-
-        @pl.when(go_left & (z < R - 1))
-        def _():
-            remote(col_sl.at[t_left], col_rl.at[t_left], pair(c_zl, t_left), row_of(z)).wait_recv()
-            col_sl[t_left] = (col_part(t_left) + col_rl[t_left].astype(jnp.float32)).astype(col_sl.dtype)
-
-        send(go_left, left)
-
-    for k in range(R - 2):
-        col_phase(k)
-        x_wait(k + 1)
-        if k + 2 < R - 1:
-            x_send(k + 2)
-    if R == 2:
-        pass
+        half = pl.ds(h * H, H)
+
+        def one(go, first, t, d, out, into, sem, dev):
+            def make(to):
+                return remote(out.at[t, half], into.at[t, half], pair(sem, t, h), to)
+
+            @pl.when(go & first)
+            def _():
+                out[t, half] = col_slot(d, h)[...].astype(out.dtype)
+
+            @pl.when(go & jnp.logical_not(first))
+            def _():
+                make(row_of(z)).wait_recv()
+                out[t, half] = (col_slot(d, h)[...] + into[t, half].astype(jnp.float32)).astype(out.dtype)
+
+            send(go, lambda: make(row_of(dev)))
+
+        one(go_right, z == 0, t_right, R - 1 - t_right, col_sr, col_rr, c_zr, z + 1)
+        one(go_left, z == R - 1, t_left, t_left, col_sl, col_rl, c_zl, z - 1)
+
+    def col_step(k):
+        for h in range(HALVES):
+            col_phase(k, h)
+
+    for k in range(R - 3):
+        col_step(k)
+        x_pass(k + 2)
     if not diag_early:
         diag_send()
 
     project(xg, PG, v, col_ids, row_ids, lhs_rows, R)
-    expand(lhs_rows, u, p_rows)
-
-    for dx in range(X):
-        xx = (mx + dx) % X
-        s1[dx] = p_rows[:, lanes_at(xx * 2 + 1 - core, Q)].astype(s1.dtype)
-        send(True, lambda dx=dx: remote(s1.at[dx], r1.at[dx], pair(r1_sem, dx), col_of(sib)))
-
-    col_phase(R - 2)
-
-    for dx in list(range(1, X)) + [0]:
+    others = [(mx + dx) % X for dx in range(1, X)]
+
+    def row_send(dx, xx):
+        lanes = lanes_at(xx * 2 + 1 - core, Q)
+        expand(lhs_rows, u, p_rows, lanes.start, Q)
+        s1[dx] = p_rows[:, lanes].astype(s1.dtype)
+        send(True, lambda: remote(s1.at[dx], r1.at[dx], pair(r1_sem, dx), col_of(sib)))
+
+    def row_wait(dx):
         remote(s1.at[dx], r1.at[dx], pair(r1_sem, dx), col_of(c)).wait_recv()
-        xx = (mx + dx) % X
-        part = p_rows[:, lanes_at(xx * 2 + core, Q)] + r1[dx].astype(jnp.float32)
-        if dx:
-            s2[dx] = part.astype(s2.dtype)
-            send(True, lambda dx=dx, xx=xx: remote(
-                s2.at[dx], r2.at[dx], pair(r2_sem, dx), col_of(xx * 2 + core)))
-        else:
-            sum3[...] = part
+
+    def across(dx, step, to):
+        rows = rows_at((z + step) % R)
+        return remote(s2.at[dx, rows], r2.at[dx, rows], pair(r2_sem, dx, step), to)
+
+    for dx, xx in enumerate(others, 1):
+        row_send(dx, xx)
+    for dx, xx in enumerate(others, 1):
+        expand(lhs_rows, u, p_rows, (xx * 2 + core) * Q, Q)
+    if R > 2:
+        col_step(R - 3)
+    for dx, xx in enumerate(others, 1):
+        row_wait(dx)
+        for step in list(range(1, R)) + [0]:
+            rows = rows_at((z + step) % R)
+            s2[dx, rows] = (
+                p_rows[rows, lanes_at(xx * 2 + core, Q)] + r1[dx, rows].astype(jnp.float32)
+            ).astype(s2.dtype)
+            send(True, lambda dx=dx, xx=xx, step=step: across(dx, step, col_of(xx * 2 + core)))
+    row_send(0, mx)
+    expand(lhs_rows, u, p_rows, c * Q, Q)
+    col_step(R - 2)
+    row_wait(0)
+    sum3[...] = p_rows[:, lanes_at(c, Q)] + r1[0].astype(jnp.float32)
 
     load_d.wait()
     pl.when(c == root)(lambda: dvec.__setitem__(..., xg[rows_at(z % PG)]))
@@ -287,30 +308,27 @@
             dvec, dvec, pair(d_sem, step), col_of(c)).wait_recv())
     diag_part = dot_nt(dvec[...], diag[...])
 
-    for dx in range(1, X):
-        remote(s2.at[dx], r2.at[dx], pair(r2_sem, dx), col_of(c)).wait_recv()
-        sum3[...] += r2[dx].astype(jnp.float32)
-    s3[...] = sum3[...].astype(s3.dtype)
-    for step in range(1, R):
+    for step in list(range(1, R)) + [0]:
         to = (z + step) % R
-        send(True, lambda step=step, to=to: remote(
-            s3.at[rows_at(to)], r3.at[rows_at(step)], pair(r3_sem, step), row_of(to)))
-
-    result = col_part(z)
-    cols_out[...] = result.astype(cols_out.dtype)
-    acc = p_cols.at[rows_at(z * W // TILE), lanes_at(z % (TILE // W), W)]
-
-    @pl.when(z > 0)
-    def _():
-        t = R - 1 - z
-        remote(col_sr.at[t], col_rr.at[t], pair(c_zr, t), row_of(z)).wait_recv()
-        acc[...] += col_rr[t].astype(jnp.float32)
-
-    @pl.when(z < R - 1)
-    def _():
-        remote(col_sl.at[z], col_rl.at[z], pair(c_zl, z), row_of(z)).wait_recv()
-        acc[...] += col_rl[z].astype(jnp.float32)
-
+        rows = rows_at(to)
+        for dx in range(1, X):
+            across(dx, step, col_of(c)).wait_recv()
+            sum3[rows] += r2[dx, rows].astype(jnp.float32)
+        if step:
+            s3[rows] = sum3[rows].astype(s3.dtype)
+            send(True, lambda step=step, to=to, rows=rows: remote(
+                s3.at[rows], r3.at[rows_at(step)], pair(r3_sem, step), row_of(to)))
+
+    acc = col_slot(z)
+    for h in range(HALVES):
+        half = pl.ds(h * H, H)
+
+        def last(t, out, into, sem):
+            remote(out.at[t, half], into.at[t, half], pair(sem, t, h), row_of(z)).wait_recv()
+            col_slot(z, h)[...] += into[t, half].astype(jnp.float32)
+
+        pl.when(z > 0)(lambda: last(R - 1 - z, col_sr, col_rr, c_zr))
+        pl.when(z < R - 1)(lambda: last(z, col_sl, col_rl, c_zl))
     cols_out[...] = acc[...].astype(cols_out.dtype)
 
     out = sum3[rows_at(z)] + diag_part
@@ -374,17 +392,17 @@
             dma((2, steps)),
             dma((2, X, R)),
             dma((2, X, R)),
-            dma((2, steps)),
-            dma((2, steps)),
+            dma((2, steps, HALVES)),
+            dma((2, steps, HALVES)),
             dma((2, C)),
-            dma((2, steps)),
-            dma((2, steps)),
+            dma((2, steps, HALVES)),
+            dma((2, steps, HALVES)),
             dma((2, X)),
-            dma((2, X)),
+            dma((2, X, R)),
             dma((2, R)),
         ],
         compiler_params=pltpu.CompilerParams(
-            collective_id=0, has_side_effects=True, vmem_limit_bytes=48 * 1024 * 1024
+            collective_id=0, has_side_effects=True, vmem_limit_bytes=60 * 1024 * 1024
         ),
         name="slab",
     )(

time: 63.7 us -> 56.2 us (0.88)
  Pallas kernels: 56.8 us -> 52.2 us
  local copies, waits for them, and re-layouts: 6.04 us -> 3.14 us
    pallas_call x1, Pallas kernels: 56.8 us -> 52.2 us  [body(): pl.pallas_call(functools.partial(kernel, (R, C, V, W, Q, TILE, PG)), out_...]
    unnamed x12 -> x2, local copies, waits for them, and re-layouts: 6.04 us -> 3.14 us
where the time goes in v2:
time: 56.2 us; the launch traced here: 56 us
  Pallas kernels  52.2 us (93%)
  local copies, waits for them, and re-layouts  3.14 us (6%)
  between operations  0.64 us (1%)
    pallas_call x1, Pallas kernels, body(): pl.pallas_call(functools.partial(kernel, (R, C, V, W, Q, TILE, PG)), out_...  52.2 us
    unnamed x2, local copies, waits for them, and re-layouts  3.14 us

profile of v2, /device:TPU:0, one launch (start us, length us, event | category | flops | bytes accessed | tf_op | source)
XLA Modules:
  0.0 56.0 jit_solution(5752761119252743247)
XLA Ops:
  0.6 52.2 %slab.1 = (bf16[64,512]{1,0:T(8,128)(2,1)}, bf16[64,2048]{1,0:T(8,128)(2,1)}) custom-call(s32[4,4]{1,0:T(4,128)} %ranks.1, s32[1,16]{1,0:T(1,128)} %order.1, bf16[64,2048]{1,0:T(8,128)(2,1)} %x_hbm.1, bf16[64,512]{1,0:T(8,128)(2,1)} %w_hbm.1, bf16[512,2048]{1,0:T(8,128)(2,1)} %diag_hbm.1, bf16[1280,2048]{1,0:T(8,128)(2,1)} %bitcast.2, bf16[1280,2048]{1,0:T(8,128)(2,1)} %bitcast.3), custom_call_target="tpu_custom_call" | custom-call | tf_op jit(solution)/shard_map/slab/pallas_call | solution.py:358
  52.8 1.5 %copy.11 = bf16[64,512]{1,0:T(8,128)(2,1)} copy(bf16[64,512]{1,0:T(8,128)(2,1)} %get-tuple-element.4) | data formatting | bytes 131072
  54.3 1.7 %copy.12 = bf16[64,2048]{1,0:T(8,128)(2,1)} copy(bf16[64,2048]{1,0:T(8,128)(2,1)} %get-tuple-element.5) | data formatting | bytes 524288
